TPU v7x, 256 devices: a whole 4x4x8 slice. The times are simulated.
256 devices in a mesh: row: 4 (over x_hi, core), col: 16 (over x_lo, z), win: 4 (over y).
Axes of the slice: x: 4 (x_hi: 2, x_lo: 2; x = x_hi * 2 + x_lo), y: 4, z: 8, core: 2. Of those that a mesh axis runs over, the one named last changes fastest.
Arguments:
- spectra: bfloat16 [8192, 8, 2, 256], P(('row', 'col', 'win')), may hold values from -110 to 110
- window_flags: bfloat16 [8192, 256], P(('row', 'col', 'win')), may hold values from 0 to 1, as said below
- station_map: int32 [8192], P(('row', 'col', 'win')), may hold values from 0 to 8191, as said below
Outputs:
- cross_spectra: bfloat16 [8, 2, 8192, 8192], P('win', None, 'row', 'col')
Inputs may be any that keep to these rules, and one draw needn't show every extreme that they name: `station_map`: each aligned block of 32 arrival positions holds a permutation of the same block's station numbers. `window_flags`: some stations have weight 0 in every window.
All inputs are finite; a program needn't handle non-finite values.
Results may differ from a plain program's by a relative error of at most 0.0057.
Values may be sent and summed in bfloat16 or wider, within the bound.
A program may use at most 128 MiB of HBM per device.

v0:
```python
import jax
import jax.numpy as jnp
from jax import lax
from jax.sharding import PartitionSpec as P

STATIONS = 8192


water_level = 0.05


def whiten(spectra, window_flags, station_map):
    amplitudes = spectra.astype(jnp.float32)
    band_power = amplitudes[:, :, 0, :] ** 2 + amplitudes[:, :, 1, :] ** 2
    mean_power = jnp.mean(band_power, axis=1, keepdims=True)
    window_mask = window_flags.astype(jnp.float32)[:, None, :]
    whitening = lax.rsqrt(band_power + mean_power + water_level) * window_mask
    whitened = (amplitudes * whitening[:, :, None, :]).astype(jnp.bfloat16)
    arrive_count = spectra.shape[0]
    positions = station_map - jnp.min(station_map)
    arrival_onehot = (positions[:, None] == jnp.arange(arrive_count)[None, :]).astype(jnp.bfloat16)
    ordered = jnp.einsum(
        "kj,kfcw->jfcw", arrival_onehot, whitened, preferred_element_type=jnp.float32
    ).astype(jnp.bfloat16)
    station_flags = jnp.einsum(
        "kj,kw->jw", arrival_onehot, window_flags, preferred_element_type=jnp.float32
    ).astype(jnp.bfloat16)
    return (ordered, station_flags)


def cross_tile(row_data, row_flags, col_data, col_flags):
    window_count = row_flags.shape[1]
    real_rows = row_data[:, :, :window_count]
    imag_rows = row_data[:, :, window_count:]
    turned_rows = jnp.concatenate([imag_rows, -real_rows], axis=2)
    left_side = jnp.stack([row_data, turned_rows], axis=0)
    pair_tile = jnp.einsum(
        "pifk,jfk->fpij", left_side, col_data, preferred_element_type=jnp.float32
    )
    counts = jnp.dot(row_flags, col_flags.T, preferred_element_type=jnp.float32)
    scaling = lax.rsqrt(jnp.maximum(counts, 1.0))
    return (pair_tile * scaling[None, None]).astype(jnp.bfloat16)


def shards(spectra, window_flags, station_map):
    ordered, station_flags = whiten(spectra, window_flags, station_map)
    win_count = lax.axis_size("win")
    arrive_count = ordered.shape[0]
    bin_count = ordered.shape[1]
    window_count = ordered.shape[3]
    merged = ordered.reshape(arrive_count, bin_count, 2 * window_count)
    flag_copies = jnp.broadcast_to(
        station_flags[:, None, :], (arrive_count, win_count, window_count)
    )
    band_rows, band_flags = (
        lax.all_to_all(merged, "win", split_axis=1, concat_axis=0, tiled=True),
        lax.all_to_all(flag_copies, "win", split_axis=1, concat_axis=0, tiled=True),
    )
    band_flags = band_flags.reshape(band_flags.shape[0], window_count)
    row_total = STATIONS // lax.axis_size("row")
    col_total = STATIONS // lax.axis_size("col")
    row_index = lax.axis_index("row")
    col_index = lax.axis_index("col")
    all_rows, all_flags = (
        lax.all_gather(band_rows, ("row", "col"), axis=0, tiled=True),
        lax.all_gather(band_flags, ("row", "col"), axis=0, tiled=True),
    )
    row_data = lax.dynamic_slice_in_dim(all_rows, row_index * row_total, row_total, 0)
    row_flags = lax.dynamic_slice_in_dim(all_flags, row_index * row_total, row_total, 0)
    col_data = lax.dynamic_slice_in_dim(all_rows, col_index * col_total, col_total, 0)
    col_flags = lax.dynamic_slice_in_dim(all_flags, col_index * col_total, col_total, 0)
    return cross_tile(row_data, row_flags, col_data, col_flags)


def solution(mesh):
    return jax.shard_map(
        shards,
        mesh=mesh,
        in_specs=(
            P(("row", "col", "win"), None, None, None),
            P(("row", "col", "win"), None),
            P(("row", "col", "win")),
        ),
        out_specs=P("win", None, "row", "col"),
        check_vma=False,
    )
```

profile of v0, /device:TPU:99, one launch (start us, length us, event | category | flops | bytes accessed | tf_op | source)
XLA Modules:
  0.0 441.9 jit_solution(17407032043259475869)
XLA Ops:
  6.5 0.0 all-gather.5.cloned.1.call-start
  6.5 1.3 reduce_min.9
  7.8 1.3 broadcast_subtract_fusion
  9.1 0.8 convolution_convert_fusion.1
  10.0 8.6 %all_to_all.33 = bf16[32,4,256]{2,0,1:T(8,128)(2,1)} all-to-all(bf16[32,4,256]{2,0,1:T(8,128)(2,1)S(1)} %broadcast_in_dim.2), channel_id=1, replica_groups=mesh['row'=4,'col'=16,'win'=4] {'win'}, dimensions={1} | all-to-all | bytes 131072 | tf_op jit(solution)/shard_map/all_to_all | solution.py:57
  18.5 0.0 all-gather.5.cloned.1.call-update
  18.6 0.0 all-gather.3.cloned.1.call-start
  18.6 0.7 convert_element_type.20
  19.3 1.0 copy_convert_fusion
  20.3 0.1 fusion.11
  20.4 0.1 multiply_bitcast_fusion
  20.5 1.0 multiply_convert_fusion.1
  21.5 0.2 fusion.4
  21.8 7.9 %all_to_all.34 = bf16[32,8,512]{2,0,1:T(8,128)(2,1)S(1)} all-to-all(bf16[32,8,512]{2,0,1:T(8,128)(2,1)S(1)} %bitcast.30), channel_id=1, replica_groups=mesh['row'=4,'col'=16,'win'=4] {'win'}, dimensions={1} | all-to-all | bytes 524288 | tf_op jit(solution)/shard_map/all_to_all | solution.py:56
  29.7 0.7 copy.16
  30.4 0.0 all-gather.3.cloned.1.call-update
  30.4 181.6 %all-gather.5.cloned.1.call-done = bf16[8192,256]{1,0:T(8,128)(2,1)} async-done(((bf16[128,256]{1,0:T(8,128)(2,1)}), bf16[8192,256]{1,0:T(8,128)(2,1)}) %all-gather.5.cloned.1.call-update) | async-done | bytes 4194320 | tf_op jit(solution)/shard_map/all_gather | solution.py:66
  212.1 4.0 maximum_rsqrt_fusion
  216.1 204.3 %all-gather.3.cloned.1.call-done = bf16[8192,2,512]{2,0,1:T(8,128)(2,1)} async-done(((bf16[128,2,512]{2,0,1:T(8,128)(2,1)}), bf16[8192,2,512]{2,0,1:T(8,128)(2,1)}) %all-gather.3.cloned.1.call-update) | async-done | bytes 16777232 | tf_op jit(solution)/shard_map/all_gather | solution.py:65
  420.3 2.7 constant_dynamic-slice_fusion
  423.1 0.0 copy-start
  423.1 2.7 maximum_bitcast_fusion
  425.8 0.7 copy-done
  426.5 8.5 %multiply_convert_fusion = bf16[2,2,2048,512]{3,2,1,0:T(8,128)(2,1)} fusion(f32[2048,512]{1,0:T(8,128)S(1)} %copy-done, bf16[8192,2,512]{2,0,1:T(8,128)(2,1)} %all-gather.3.cloned.1.call-done, s32[]{:T(128)S(6)} %select_n.9, bf16[1,2048,2,512]{3,1,2,0:T(8,128)(2,1)S(1)} %get-tuple-element.7, bf16[1,2048,2,512]{3,1,2,0:T(8,128)(2,1)S(1)} %get-tuple-element.8), kind=kOutput, calls=%fused_computation | convolution fusion | flops 4307550208 | bytes 22020100 | tf_op jit(solution)/shard_map/pifk,jfk->fpij/dot_general | solution.py:37
  (3 shorter events, 0.0 us)
Async XLA Ops:
  6.5 205.5 %all-gather.5.cloned.1.call-start = ((), (), s32[]{:S(2)}) async-start(), calls=%async_computation.3 | async-start | bytes 4259840 | tf_op jit(solution)/shard_map/all_gather | solution.py:66
  18.6 401.8 %all-gather.3.cloned.1.call-start = ((), (), s32[]{:S(2)}) async-start(), calls=%async_computation.2 | async-start | bytes 17039360 | tf_op jit(solution)/shard_map/all_gather | solution.py:65
  423.1 3.5 copy-start
Sparse Core Ops, SparseCore 0:
  18.7 193.3 all-gather.4
  213.9 206.4 all-gather.2
where the time goes:
time: 442 us
  waiting for transfers between devices  386 us (87%)
  blocking collectives  16.5 us (4%)
  matrix products  13.6 us (3%)
  between operations  13.5 us (3%)
  other arithmetic  10.9 us (2%)
    all_gather x1, waiting for transfers between devices, shards(): lax.all_gather(band_rows, ('row', 'col'), axis=0, tiled=True)  204 us
    all_gather x1, waiting for transfers between devices, shards(): lax.all_gather(band_flags, ('row', 'col'), axis=0, tiled=True)  182 us
  transfers between devices with their start and end apart: 2, of which 2 were waited for; matrix products, arithmetic and copies ran while one was open for 2% of the time, Pallas kernels for 0%

commit v1 on v0

v1 whole, which is shorter than its diff:
```python
import jax
import jax.numpy as jnp
from jax import lax
from jax.experimental import pallas as pl
from jax.experimental.pallas import tpu as pltpu
from jax.sharding import PartitionSpec as P

MESH = pl.DeviceIdType.MESH
WATER_LEVEL = 0.05
NT = (((1,), (1,)), ((), ()))
ORDER = (
    "F1", "O0", "F2", "O1", "A1a", "F3", "A1b", "P0", "FX", "B1", "X0", "A2",
    "FY", "P1", "X1", "R0", "S0", "B2", "A3", "X2", "R1", "S1", "P2", "FH",
    "X3", "R2", "B3", "A4", "FR", "S2", "P3", "W0", "X4", "R3", "B4", "P4",
    "S3", "R4", "E0", "T0", "M01", "S4", "M14", "E1",
)


def turn_columns(cols_ref, b, sides):
    both = cols_ref[b].reshape(512, 512)
    sides[:512, :] = both
    sides[512:, :256] = -both[:, 256:]
    sides[512:, 256:] = both[:, :256]


def pair_part(rows_ref, b, sides, scaling, n):
    tile = lax.dot_general(
        rows_ref[b].reshape(2048, 512), sides[pl.ds(pl.multiple_of(n * 256, 256), 256), :], NT,
        preferred_element_type=jnp.float32,
    )
    return (tile * scaling[:, part_of(n)]).astype(jnp.bfloat16)


def part_of(n):
    return pl.ds(pl.multiple_of((n % 2) * 256, 256), 256)


def gather_kernel(
    spec_ref, flag_ref, map_ref, rows, cols, scaling, first,
    row_flags, col_flags, staged, sides, flag_in, map_in, in_sem,
    ex_send, ex_recv, z_send, z_recv, x_send, x_recv,
    f_send, f_recv, fx_send, fx_recv, fy_send, fy_recv,
    c_send, c_recv, c_copy, d_send, fc_send, fc_recv, fc_copy, fd_send,
):
    flag_copy = pltpu.make_async_copy(flag_ref, flag_in, in_sem.at[0])
    map_copy = pltpu.make_async_copy(map_ref, map_in, in_sem.at[1])
    map_copy.start()
    flag_copy.start()
    r = lax.axis_index("row")
    c = lax.axis_index("col")
    y = lax.axis_index("win")
    x_hi, core = r // 2, r % 2
    x_lo, z = c // 8, c % 8
    x = x_hi * 2 + x_lo
    other_lo = 1 - x_lo

    def device(xx, cc, zz, yy):
        return {"row": (xx // 2) * 2 + cc, "col": (xx % 2) * 8 + zz, "win": yy}

    z_ids = (device(x, core, (z + 1) % 8, y), device(x, core, (z + 7) % 8, y))
    y_at = ((y // 2) * 2 + 1 - y % 2, (y + 2) % 4, 3 - y)
    y_ids = tuple(device(x, core, z, yy) for yy in y_at)
    x_id = device(x_hi * 2 + other_lo, core, z, y)
    cross_id = device(3 - x, core, z, y)
    twin_id = device(x, 1 - core, z, y)

    barrier = pltpu.get_barrier_semaphore()
    for target in (*z_ids, *y_ids, x_id, cross_id, twin_id):
        pl.semaphore_signal(barrier, inc=1, device_id=target, device_id_type=MESH)

    total = jnp.zeros((32, 256), jnp.float32)
    for f in range(8):
        re = spec_ref[:, f * 512:f * 512 + 256].astype(jnp.float32)
        im = spec_ref[:, f * 512 + 256:f * 512 + 512].astype(jnp.float32)
        total += re * re + im * im
    mean = total * 0.125
    map_copy.wait()
    flag_copy.wait()
    arrival = lax.broadcasted_iota(jnp.int32, (32, 32), 0)
    onehot = jnp.where(arrival == (map_in[...] % 32), 1.0, 0.0).astype(jnp.bfloat16)
    flags = flag_in[...]
    ordered_flags = jnp.dot(onehot, flags, preferred_element_type=jnp.float32)
    row_flags[c, y] = ordered_flags.astype(jnp.bfloat16)
    mask = flags.astype(jnp.float32)
    for f in range(8):
        re = spec_ref[:, f * 512:f * 512 + 256].astype(jnp.float32)
        im = spec_ref[:, f * 512 + 256:f * 512 + 512].astype(jnp.float32)
        gain = lax.rsqrt(re * re + im * im + mean + WATER_LEVEL) * mask
        white = jnp.concatenate([re * gain, im * gain], axis=1).astype(jnp.bfloat16)
        staged[f // 2, f % 2] = jnp.dot(
            onehot, white, preferred_element_type=jnp.float32
        ).astype(jnp.bfloat16)
    for b in range(2):
        rows[b, c, pl.ds(y * 32, 32), :] = staged[y, b]

    pl.semaphore_wait(barrier, 8)

    started = []

    def remote(src, dst, send, recv, target):
        copy = pltpu.make_async_remote_copy(
            src_ref=src, dst_ref=dst, send_sem=send, recv_sem=recv,
            device_id=target, device_id_type=MESH,
        )
        copy.start()
        started.append(copy)

    def await_recv(dst, recv):
        pltpu.make_async_remote_copy(
            src_ref=dst, dst_ref=dst, send_sem=recv, recv_sem=recv,
            device_id=twin_id, device_id_type=MESH,
        ).wait_recv()

    def z_from(s, k):
        return (z + (8 - k if s == 0 else k)) % 8

    def flag_at(s, k):
        return row_flags.at[x_lo * 8 + z_from(s, k), y]

    def flag_go(s, k):
        remote(flag_at(s, k), flag_at(s, k), f_send.at[s, k], f_recv.at[s, k], z_ids[s])

    def flag_wait(s, k):
        await_recv(flag_at(s, k), f_recv.at[s, k - 1])

    def exchange(b, i):
        remote(
            staged.at[y_at[i], b], rows.at[b, c, pl.ds(y * 32, 32)],
            ex_send.at[b, i], ex_recv.at[b, i], y_ids[i],
        )

    def exchange_wait(b, i):
        await_recv(rows.at[b, c, pl.ds(y_at[i] * 32, 32)], ex_recv.at[b, i])

    exchange(0, 0)
    exchange(1, 0)
    flag_go(0, 0)
    flag_go(1, 0)
    for b in range(2):
        exchange(b, 1)
        exchange(b, 2)

    kind_bin = (0, 1, 1)

    def half_start(q):
        return (y // 2 if q == 0 else 1 - y // 2) * 64

    def half_of(b, lane, zz, q):
        return rows.at[b, lane * 8 + zz, pl.ds(half_start(q), 64)]

    def lane_of(kind):
        return other_lo if kind == 2 else x_lo

    def sides_of(k, q):
        return (0, 1) if k < 4 else (q,)

    def z_ref(kind, s, k, q):
        return half_of(kind_bin[kind], lane_of(kind), z_from(s, k), q)

    def z_go(kind, s, k, q):
        if k < 3 or s == q:
            ref = z_ref(kind, s, k, q)
            remote(ref, ref, z_send.at[kind, s, k, q], z_recv.at[kind, s, k, q], z_ids[s])

    def z_go_both(kind, q):
        for s in range(2):
            z_go(kind, s, 0, q)

    def z_step(kind, k, q):
        for s in sides_of(k, q):
            await_recv(z_ref(kind, s, k, q), z_recv.at[kind, s, k - 1, q])
            if k < 4:
                z_go(kind, s, k, q)

    def x_slots(k):
        return ((1, 0),) if k == 0 else ((2 * k, 0), (2 * k + 1, 1)) if k < 4 else ((8, 0),)

    def x_go(b, slot, zz, q):
        ref = half_of(b, x_lo, zz, q)
        remote(ref, ref, x_send.at[slot, q], x_recv.at[slot, q], x_id)

    def x_wait(b, slot, zz, q):
        await_recv(half_of(b, other_lo, zz, q), x_recv.at[slot, q])

    primary = core == z // 4
    inner = (x == 0) | (x == 3)
    want_lane = (z % 4) // 2
    want_half = z % 2
    hand_id = device(jnp.where(inner, x, 3 - x), jnp.where(inner, 1 - core, core), z, y)

    def col_half(b, j, q):
        return cols.at[b, j, pl.ds(half_start(q), 64)]

    def hand_copy(b, lane, zz, q):
        j = zz % 4
        return pltpu.make_async_remote_copy(
            src_ref=half_of(b, lane, zz, q), dst_ref=col_half(b, j, q),
            send_sem=c_send.at[b, j, q], recv_sem=c_recv.at[b, j, q],
            device_id=hand_id, device_id_type=MESH,
        )

    def local_copy(b, lane, zz, q):
        j = zz % 4
        return pltpu.make_async_copy(half_of(b, lane, zz, q), col_half(b, j, q), c_copy.at[b, j, q])

    def hand(b, lane, k, q):
        for s in range(1 if k in (0, 4) else 2):
            zz = z_from(s, k)

            @pl.when(primary & (lane == want_lane) & (zz // 4 == want_half))
            def _():
                hand_copy(b, lane, zz, q).start()

                @pl.when(inner)
                def _():
                    local_copy(b, lane, zz, q).start()

    relay = primary & (x != 0) & (x != 3)
    secondary = core != z // 4

    def relay_copy(b, j, q):
        return pltpu.make_async_remote_copy(
            src_ref=col_half(b, j, q), dst_ref=col_half(b, j, q), send_sem=d_send.at[b, j, q],
            recv_sem=c_recv.at[b, j, q], device_id=twin_id, device_id_type=MESH,
        )

    def pass_on(b, k):
        for q in range(2):
            for s in range(1 if k in (0, 4) else 2):
                zz = z_from(s, k)

                @pl.when(relay & (zz // 4 == want_half))
                def _():
                    await_recv(col_half(b, zz % 4, q), c_recv.at[b, zz % 4, q])
                    relay_copy(b, zz % 4, q).start()

    def step(kind, k, q):
        z_step(kind, k, q)
        if kind == 0:
            for slot, s in x_slots(k):
                x_go(0, slot, z_from(s, k), q)
        hand(kind_bin[kind], lane_of(kind), k, q)

    def x_step(k):
        for q in range(2):
            for slot, s in x_slots(k):
                x_wait(0, slot, z_from(s, k), q)
            hand(0, other_lo, k, q)

    def both(kind, k):
        for q in range(2):
            step(kind, k, q)

    def open_half(q):
        for b in range(2):
            for i in (0,) if q == 0 else (1, 2):
                exchange_wait(b, i)
            z_go_both(b, q)
        x_go(1, 0, z, q)
        x_go(0, 1, z, q)
        hand(0, x_lo, 0, q)
        hand(1, x_lo, 0, q)

    def open_other(q):
        x_wait(1, 0, z, q)
        z_go_both(2, q)
        hand(1, other_lo, 0, q)

    def flag_step(k):
        for s in range(2):
            flag_wait(s, k)
            if k < 3:
                flag_go(s, k)
        if k == 3:
            flag_go(0, 3)

    def flags_x():
        flag_wait(0, 4)
        lane_flags = row_flags.at[pl.ds(x_lo * 8, 8), y]
        remote(lane_flags, lane_flags, fx_send.at[0], fx_recv.at[0], x_id)
        for i in range(3):
            remote(lane_flags, lane_flags, fy_send.at[0, i], fy_recv.at[0, i], y_ids[i])

    def flags_y():
        far_flags = row_flags.at[pl.ds(other_lo * 8, 8), y]
        await_recv(far_flags, fx_recv.at[0])
        for i in range(3):
            remote(far_flags, far_flags, fy_send.at[1, i], fy_recv.at[1, i], y_ids[i])

    flag_src = row_flags.at[pl.ds((z % 4) * 4, 4)]
    flag_hand = pltpu.make_async_remote_copy(
        src_ref=flag_src, dst_ref=col_flags, send_sem=fc_send.at[0], recv_sem=fc_recv.at[0],
        device_id=hand_id, device_id_type=MESH,
    )
    flag_local = pltpu.make_async_copy(flag_src, col_flags, fc_copy.at[0])
    flag_relay = pltpu.make_async_remote_copy(
        src_ref=col_flags, dst_ref=col_flags, send_sem=fd_send.at[0], recv_sem=fc_recv.at[0],
        device_id=twin_id, device_id_type=MESH,
    )

    def flags_hand():
        for lane in range(2):
            for i in range(3):
                base = x_lo * 8 if lane == 0 else other_lo * 8
                await_recv(row_flags.at[pl.ds(base, 8), y_at[i]], fy_recv.at[lane, i])

        @pl.when(primary)
        def _():
            flag_hand.start()

            @pl.when(inner)
            def _():
                flag_local.start()

    def flags_pass():
        @pl.when(relay)
        def _():
            await_recv(col_flags, fc_recv.at[0])
            flag_relay.start()

    def settle(b):
        @pl.when(secondary)
        def _():
            for j in range(4):
                for q in range(2):
                    await_recv(col_half(b, j, q), c_recv.at[b, j, q])

        @pl.when(primary & inner)
        def _():
            for j in range(4):
                for q in range(2):
                    local_copy(b, want_lane, want_half * 4 + j, q).wait()

    def weights():
        @pl.when(secondary)
        def _():
            await_recv(col_flags, fc_recv.at[0])

        @pl.when(primary & inner)
        def _():
            flag_local.wait()

        for half in range(2):
            counts = lax.dot_general(
                row_flags[...].reshape(2048, 256), col_flags[2 * half:2 * half + 2].reshape(256, 256), NT,
                preferred_element_type=jnp.float32,
            )
            scaling[:, half * 256:(half + 1) * 256] = lax.rsqrt(jnp.maximum(counts, 1.0))

    def tile(n):
        first[n // 2, :, part_of(n)] = pair_part(rows, 0, sides, scaling, n)

    flag_steps = {
        "F1": lambda: flag_step(1), "F2": lambda: flag_step(2), "F3": lambda: flag_step(3),
        "FX": flags_x, "FY": flags_y, "FH": flags_hand, "FR": flags_pass, "W0": weights,
    }
    for token in ORDER:
        kind, k = token[0], token[1]
        if kind in "FW":
            flag_steps[token]()
        elif kind == "E":
            settle(int(k))
        elif kind == "T":
            turn_columns(cols, 0, sides)
        elif kind == "M":
            pl.loop(int(k), int(token[2]))(tile)
        elif kind == "O":
            open_half(int(k))
        elif kind == "X":
            x_step(int(k))
        elif kind in "RS":
            pass_on("RS".index(kind), int(k))
        else:
            for q in ("ab".index(token[2]),) if len(token) > 2 else (0, 1):
                if kind == "P" and k == "0":
                    open_other(q)
                else:
                    step("ABP".index(kind), int(k), q)

    for copy in started:
        copy.wait_send()

    @pl.when(primary)
    def _():
        flag_hand.wait_send()
        for b in range(2):
            for j in range(4):
                for q in range(2):
                    hand_copy(b, want_lane, want_half * 4 + j, q).wait_send()

    @pl.when(relay)
    def _():
        flag_relay.wait_send()
        for b in range(2):
            for j in range(4):
                for q in range(2):
                    relay_copy(b, j, q).wait_send()


def gather(spectra, window_flags, station_map):
    vmem = pl.BlockSpec(memory_space=pltpu.VMEM)
    hbm = pl.BlockSpec(memory_space=pltpu.HBM)
    dma = pltpu.SemaphoreType.DMA
    return pl.pallas_call(
        gather_kernel,
        out_shape=(
            jax.ShapeDtypeStruct((2, 16, 128, 512), jnp.bfloat16),
            jax.ShapeDtypeStruct((2, 4, 128, 512), jnp.bfloat16),
            jax.ShapeDtypeStruct((2048, 512), jnp.float32),
            jax.ShapeDtypeStruct((2, 2048, 512), jnp.bfloat16),
        ),
        in_specs=[vmem, hbm, hbm],
        out_specs=(vmem,) * 4,
        scratch_shapes=[
            pltpu.VMEM((16, 4, 32, 256), jnp.bfloat16),
            pltpu.VMEM((4, 4, 32, 256), jnp.bfloat16),
            pltpu.VMEM((4, 2, 32, 512), jnp.bfloat16),
            pltpu.VMEM((1024, 512), jnp.bfloat16),
            pltpu.VMEM((32, 256), jnp.bfloat16),
            pltpu.VMEM((1, 32), jnp.int32),
            dma((2,)),
            dma((2, 3)), dma((2, 3)),
            dma((3, 2, 4, 2)), dma((3, 2, 4, 2)),
            dma((9, 2)), dma((9, 2)),
            dma((2, 4)), dma((2, 4)),
            dma((1,)), dma((1,)),
            dma((2, 3)), dma((2, 3)),
            dma((2, 4, 2)), dma((2, 4, 2)), dma((2, 4, 2)), dma((2, 4, 2)),
            dma((1,)), dma((1,)), dma((1,)), dma((1,)),
        ],
        compiler_params=pltpu.CompilerParams(
            collective_id=0, has_side_effects=True, vmem_limit_bytes=32 << 20
        ),
        name="gather_rows",
    )(spectra, window_flags, station_map)


def finish_kernel(rows, cols, scaling, first, out, sides, second, sems):
    done = pltpu.make_async_copy(first, out.at[0], sems.at[0])
    done.start()
    turn_columns(cols, 1, sides)

    def copy_out(n):
        return pltpu.make_async_copy(
            second.at[n // 2, :, part_of(n)], out.at[1, n // 2, :, part_of(n)], sems.at[1 + n]
        )

    @pl.loop(0, 4)
    def _(n):
        second[n // 2, :, part_of(n)] = pair_part(rows, 1, sides, scaling, n)
        copy_out(n).start()

    done.wait()
    for n in range(4):
        copy_out(n).wait()


def finish(rows, cols, scaling, first):
    vmem = pl.BlockSpec(memory_space=pltpu.VMEM)
    return pl.pallas_call(
        finish_kernel,
        out_shape=jax.ShapeDtypeStruct((2, 2, 2048, 512), jnp.bfloat16),
        in_specs=[vmem] * 4,
        out_specs=pl.BlockSpec(memory_space=pltpu.HBM),
        scratch_shapes=[
            pltpu.VMEM((1024, 512), jnp.bfloat16),
            pltpu.VMEM((2, 2048, 512), jnp.bfloat16),
            pltpu.SemaphoreType.DMA((5,)),
        ],
        compiler_params=pltpu.CompilerParams(vmem_limit_bytes=24 << 20),
        name="finish_pairs",
    )(rows, cols, scaling, first)


def run_gather(spectra, window_flags, station_map):
    flat = spectra.reshape(32, 4096)
    return gather(
        flat, pltpu.with_memory_space_constraint(window_flags, pltpu.HBM),
        pltpu.with_memory_space_constraint(station_map.reshape(1, 32), pltpu.HBM),
    )


def shards(spectra, window_flags, station_map):
    return finish(*run_gather(spectra, window_flags, station_map))


def solution(mesh):
    return jax.shard_map(
        shards,
        mesh=mesh,
        in_specs=(
            P(("row", "col", "win"), None, None, None),
            P(("row", "col", "win"), None),
            P(("row", "col", "win")),
        ),
        out_specs=P("win", None, "row", "col"),
        check_vma=False,
    )
```

time: 442 us -> 58.1 us (0.13)
  the two profiles are of different devices: /device:TPU:99 before, /device:TPU:37 now
where the time goes in v1:
time: 58.1 us; the launch traced here: 58 us
  Pallas kernels  56.8 us (98%)
  local copies, waits for them, and re-layouts  1.13 us (2%)
    pallas_call x1, Pallas kernels, gather(): pl.pallas_call(gather_kernel, out_shape=(jax.ShapeDtypeStruct((2, 16, 128...  52.7 us
    pallas_call x1, Pallas kernels, finish(): pl.pallas_call(finish_kernel, out_shape=jax.ShapeDtypeStruct((2, 2, 2048,...  4.08 us

profile of v1, /device:TPU:37, one launch (start us, length us, event | category | flops | bytes accessed | tf_op | source)
XLA Modules:
  0.0 58.0 jit_solution(12466806648402425082)
XLA Ops:
  0.0 1.1 %reshape.6.spec_ref = bf16[32,4096]{1,0:T(8,128)(2,1)S(1)} reshape(bf16[32,8,2,256]{3,2,1,0:T(2,128)(2,1)} %param.3) | data formatting | bytes 524288 | tf_op jit(solution)/shard_map/reshape | solution.py:476
  1.1 52.7 %gather_rows.1 = (bf16[2,16,128,512]{3,2,1,0:T(8,128)(2,1)S(1)}, bf16[2,4,128,512]{3,2,1,0:T(8,128)(2,1)S(1)}, f32[2048,512]{1,0:T(8,128)S(1)}, bf16[2,2048,512]{2,1,0:T(8,128)(2,1)S(1)}) custom-call(bf16[32,4096]{1,0:T(8,128)(2,1)S(1)} %reshape.6.spec_ref, bf16[32,256]{1,0:T(8,128)(2,1)} %flag_ref.1, s32[1,32]{1,0:T(1,128)} %bitcast.1), custom_call_target="tpu_custom_call" | custom-call | tf_op jit(solution)/shard_map/gather_rows/pallas_call | solution.py:404
  53.9 4.1 %finish_pairs.1 = bf16[2,2,2048,512]{3,2,1,0:T(8,128)(2,1)} custom-call(bf16[2,16,128,512]{3,2,1,0:T(8,128)(2,1)S(1)} %get-tuple-element.9.rows, bf16[2,4,128,512]{3,2,1,0:T(8,128)(2,1)S(1)} %get-tuple-element.10.cols, f32[2048,512]{1,0:T(8,128)S(1)} %get-tuple-element.11.scaling, bf16[2,2048,512]{2,1,0:T(8,128)(2,1)S(1)} %get-tuple-element.12.first), custom_call_target="tpu_custom_call" | custom-call | tf_op jit(solution)/shard_map/finish_pairs/pallas_call | solution.py:460

commit v2 on v1

--- a/solution.py
+++ b/solution.py
@@ -10,8 +10,8 @@
 NT = (((1,), (1,)), ((), ()))
 ORDER = (
     "F1", "O0", "F2", "O1", "A1a", "F3", "A1b", "P0", "FX", "B1", "X0", "A2",
-    "FY", "P1", "X1", "R0", "S0", "B2", "A3", "X2", "R1", "S1", "P2", "FH",
-    "X3", "R2", "B3", "A4", "FR", "S2", "P3", "W0", "X4", "R3", "B4", "P4",
+    "FY", "P1", "X1", "R0", "S0", "B2", "A3", "X2", "FH", "R1", "S1", "P2",
+    "X3", "FR", "R2", "B3", "A4", "S2", "P3", "W0", "X4", "R3", "B4", "P4",
     "S3", "R4", "E0", "T0", "M01", "S4", "M14", "E1",
 )
 
@@ -38,7 +38,7 @@
 def gather_kernel(
     spec_ref, flag_ref, map_ref, rows, cols, scaling, first,
     row_flags, col_flags, staged, sides, flag_in, map_in, in_sem,
-    ex_send, ex_recv, z_send, z_recv, x_send, x_recv,
+    ex_send, ex_recv, zo_send, zo_recv, xo_send, xo_recv, z_send, z_recv, x_send, x_recv,
     f_send, f_recv, fx_send, fx_recv, fy_send, fy_recv,
     c_send, c_recv, c_copy, d_send, fc_send, fc_recv, fc_copy, fd_send,
 ):
@@ -132,11 +132,19 @@
     def exchange_wait(b, i):
         await_recv(rows.at[b, c, pl.ds(y_at[i] * 32, 32)], ex_recv.at[b, i])
 
+    def quarter(b, lane, zz, i):
+        return rows.at[b, lane * 8 + zz, pl.ds((y if i == 0 else y_at[0]) * 32, 32)]
+
+    flag_go(0, 0)
+    flag_go(1, 0)
     exchange(0, 0)
     exchange(1, 0)
-    flag_go(0, 0)
-    flag_go(1, 0)
     for b in range(2):
+        own = quarter(b, x_lo, z, 0)
+        for s in range(2):
+            remote(own, own, zo_send.at[b, s], zo_recv.at[b, s], z_ids[s])
+        far = quarter(1 - b, x_lo, z, 0)
+        remote(far, far, xo_send.at[b], xo_recv.at[b], x_id)
         exchange(b, 1)
         exchange(b, 2)
 
@@ -159,7 +167,8 @@
 
     def z_go(kind, s, k, q):
         if k < 3 or s == q:
-            ref = z_ref(kind, s, k, q)
+            opening = kind < 2 and k == 0 and q == 0
+            ref = quarter(kind, x_lo, z, 1) if opening else z_ref(kind, s, k, q)
             remote(ref, ref, z_send.at[kind, s, k, q], z_recv.at[kind, s, k, q], z_ids[s])
 
     def z_go_both(kind, q):
@@ -168,7 +177,11 @@
 
     def z_step(kind, k, q):
         for s in sides_of(k, q):
-            await_recv(z_ref(kind, s, k, q), z_recv.at[kind, s, k - 1, q])
+            if kind < 2 and k == 1 and q == 0:
+                await_recv(quarter(kind, x_lo, z_from(s, 1), 0), zo_recv.at[kind, s])
+                await_recv(quarter(kind, x_lo, z_from(s, 1), 1), z_recv.at[kind, s, 0, 0])
+            else:
+                await_recv(z_ref(kind, s, k, q), z_recv.at[kind, s, k - 1, q])
             if k < 4:
                 z_go(kind, s, k, q)
 
@@ -176,11 +189,15 @@
         return ((1, 0),) if k == 0 else ((2 * k, 0), (2 * k + 1, 1)) if k < 4 else ((8, 0),)
 
     def x_go(b, slot, zz, q):
-        ref = half_of(b, x_lo, zz, q)
+        ref = quarter(b, x_lo, z, 1) if slot < 2 and q == 0 else half_of(b, x_lo, zz, q)
         remote(ref, ref, x_send.at[slot, q], x_recv.at[slot, q], x_id)
 
     def x_wait(b, slot, zz, q):
-        await_recv(half_of(b, other_lo, zz, q), x_recv.at[slot, q])
+        if slot < 2 and q == 0:
+            await_recv(quarter(b, other_lo, z, 0), xo_recv.at[slot])
+            await_recv(quarter(b, other_lo, z, 1), x_recv.at[slot, 0])
+        else:
+            await_recv(half_of(b, other_lo, zz, q), x_recv.at[slot, q])
 
     primary = core == z // 4
     inner = (x == 0) | (x == 3)
@@ -340,12 +357,13 @@
         def _():
             flag_local.wait()
 
-        for half in range(2):
+        @pl.loop(0, 2)
+        def _(half):
             counts = lax.dot_general(
-                row_flags[...].reshape(2048, 256), col_flags[2 * half:2 * half + 2].reshape(256, 256), NT,
+                row_flags[...].reshape(2048, 256), col_flags[pl.ds(2 * half, 2)].reshape(256, 256), NT,
                 preferred_element_type=jnp.float32,
             )
-            scaling[:, half * 256:(half + 1) * 256] = lax.rsqrt(jnp.maximum(counts, 1.0))
+            scaling[:, part_of(half)] = lax.rsqrt(jnp.maximum(counts, 1.0))
 
     def tile(n):
         first[n // 2, :, part_of(n)] = pair_part(rows, 0, sides, scaling, n)
@@ -420,6 +438,7 @@
             pltpu.VMEM((1, 32), jnp.int32),
             dma((2,)),
             dma((2, 3)), dma((2, 3)),
+            dma((2, 2)), dma((2, 2)), dma((2,)), dma((2,)),
             dma((3, 2, 4, 2)), dma((3, 2, 4, 2)),
             dma((9, 2)), dma((9, 2)),
             dma((2, 4)), dma((2, 4)),

time: 58.1 us -> 58.8 us (1.012)
  Pallas kernels: 56.8 us -> 57.5 us
    pallas_call x1, Pallas kernels: 52.7 us -> 53.4 us  [gather(): pl.pallas_call(gather_kernel, out_shape=(jax.ShapeDtypeStruct((2, 16, 128...]
where the time goes in v2:
time: 58.8 us; the launch traced here: 58.6 us
  Pallas kernels  57.5 us (98%)
  local copies, waits for them, and re-layouts  1.13 us (2%)
    pallas_call x1, Pallas kernels, gather(): pl.pallas_call(gather_kernel, out_shape=(jax.ShapeDtypeStruct((2, 16, 128...  53.4 us
    pallas_call x1, Pallas kernels, finish(): pl.pallas_call(finish_kernel, out_shape=jax.ShapeDtypeStruct((2, 2, 2048,...  4.06 us

profile of v2, /device:TPU:37, one launch (start us, length us, event | category | flops | bytes accessed | tf_op | source)
XLA Modules:
  0.0 58.6 jit_solution(6586516109838449518)
XLA Ops:
  0.0 1.1 %reshape.6.spec_ref = bf16[32,4096]{1,0:T(8,128)(2,1)S(1)} reshape(bf16[32,8,2,256]{3,2,1,0:T(2,128)(2,1)} %param.3) | data formatting | bytes 524288 | tf_op jit(solution)/shard_map/reshape | solution.py:495
  1.1 53.4 %gather_rows.1 = (bf16[2,16,128,512]{3,2,1,0:T(8,128)(2,1)S(1)}, bf16[2,4,128,512]{3,2,1,0:T(8,128)(2,1)S(1)}, f32[2048,512]{1,0:T(8,128)S(1)}, bf16[2,2048,512]{2,1,0:T(8,128)(2,1)S(1)}) custom-call(bf16[32,4096]{1,0:T(8,128)(2,1)S(1)} %reshape.6.spec_ref, bf16[32,256]{1,0:T(8,128)(2,1)} %flag_ref.1, s32[1,32]{1,0:T(1,128)} %bitcast.1), custom_call_target="tpu_custom_call" | custom-call | tf_op jit(solution)/shard_map/gather_rows/pallas_call | solution.py:422
  54.6 4.1 %finish_pairs.1 = bf16[2,2,2048,512]{3,2,1,0:T(8,128)(2,1)} custom-call(bf16[2,16,128,512]{3,2,1,0:T(8,128)(2,1)S(1)} %get-tuple-element.9.rows, bf16[2,4,128,512]{3,2,1,0:T(8,128)(2,1)S(1)} %get-tuple-element.10.cols, f32[2048,512]{1,0:T(8,128)S(1)} %get-tuple-element.11.scaling, bf16[2,2048,512]{2,1,0:T(8,128)(2,1)S(1)} %get-tuple-element.12.first), custom_call_target="tpu_custom_call" | custom-call | tf_op jit(solution)/shard_map/finish_pairs/pallas_call | solution.py:479
